TPU v7x, 32 devices: a whole 2x2x4 slice. The times are simulated.
32 devices in a mesh: dp: 8 (over y, x, core), tensor: 4 (over z).
Axes of the slice: x: 2, y: 2, z: 4, core: 2. Of those that a mesh axis runs over, the one named last changes fastest.
Arguments:
- tokens: bfloat16 [16384, 1024], P(('dp', 'tensor')), may hold values from -6 to 6
- out_grad: bfloat16 [16384, 1024], P(('dp', 'tensor')), may hold values from -6 to 6
- seq_lengths: int32 [8, 8], P('dp'), may hold values from 1 to 1024, 2048 in all within a row
- master_qkv: float32 [1024, 3, 1024], P('dp', None, 'tensor'), may hold values from -0.1875 to 0.1875
- first_qkv: float32 [1024, 3, 1024], P('dp', None, 'tensor'), may hold values from -24 to 24
- second_qkv: float32 [1024, 3, 1024], P('dp', None, 'tensor'), may hold values from 1.47456 to 5.89824
- master_mix: float32 [1024, 1024], P('dp', 'tensor'), may hold values from -0.1875 to 0.1875
- first_mix: float32 [1024, 1024], P('dp', 'tensor'), may hold values from -80 to 80
- second_mix: float32 [1024, 1024], P('dp', 'tensor'), may hold values from 16.384 to 65.536
- master_up: float32 [1024, 4096], P('dp', 'tensor'), may hold values from -0.35625 to 0.35625
- first_up: float32 [1024, 4096], P('dp', 'tensor'), may hold values from -24 to 24
- second_up: float32 [1024, 4096], P('dp', 'tensor'), may hold values from 1.47456 to 5.89824
- master_down: float32 [1024, 4096], P('dp', 'tensor'), may hold values from -0.09375 to 0.09375
- first_down: float32 [1024, 4096], P('dp', 'tensor'), may hold values from -80 to 80
- second_down: float32 [1024, 4096], P('dp', 'tensor'), may hold values from 16.384 to 65.536
- master_norms: float32 [6, 1024], replicated, may hold values from -1.2 to 2.02
- first_norms: float32 [6, 1024], replicated, may hold values from -80 to 80
- second_norms: float32 [6, 1024], replicated, may hold values from 16.384 to 65.536
- master_midnorm: float32 [2, 4096], replicated, may hold values from -1.2 to 2.02
- first_midnorm: float32 [2, 4096], replicated, may hold values from -40 to 40
- second_midnorm: float32 [2, 4096], replicated, may hold values from 4.096 to 16.384
- master_heads: float32 [16], replicated, may hold values from 0.5 to 2
- first_heads: float32 [16], replicated, may hold values from -640 to 640
- second_heads: float32 [16], replicated, may hold values from 1048.576 to 4194.304
Outputs:
- layer_out: bfloat16 [16384, 1024], P(('dp', 'tensor'))
- input_grad: float32 [16384, 1024], P(('dp', 'tensor'))
- updated_qkv: float32 [1024, 3, 1024], P('dp', None, 'tensor')
- moment_qkv: float32 [1024, 3, 1024], P('dp', None, 'tensor')
- square_qkv: float32 [1024, 3, 1024], P('dp', None, 'tensor')
- updated_mix: float32 [1024, 1024], P('dp', 'tensor')
- moment_mix: float32 [1024, 1024], P('dp', 'tensor')
- square_mix: float32 [1024, 1024], P('dp', 'tensor')
- updated_up: float32 [1024, 4096], P('dp', 'tensor')
- moment_up: float32 [1024, 4096], P('dp', 'tensor')
- square_up: float32 [1024, 4096], P('dp', 'tensor')
- updated_down: float32 [1024, 4096], P('dp', 'tensor')
- moment_down: float32 [1024, 4096], P('dp', 'tensor')
- square_down: float32 [1024, 4096], P('dp', 'tensor')
- updated_norms: float32 [6, 1024], replicated
- moment_norms: float32 [6, 1024], replicated
- square_norms: float32 [6, 1024], replicated
- updated_midnorm: float32 [2, 4096], replicated
- moment_midnorm: float32 [2, 4096], replicated
- square_midnorm: float32 [2, 4096], replicated
- updated_heads: float32 [16], replicated
- moment_heads: float32 [16], replicated
- square_heads: float32 [16], replicated
Inputs may be any that keep to these rules, and one draw needn't show every extreme that they name: `seq_lengths`: row g lists, in order, the lengths of the 8 sequences packed into data group g's 2048 token slots; each row sums to 2048 and holds one sequence of exactly 1024 tokens.
All inputs are finite; a program needn't handle non-finite values.
Results may differ from a plain program's by a relative error of at most 0.012.
The roundings to bfloat16 on the way count: a program that leaves them out, or rounds other values in their place, can miss the bound.
Values may be sent and summed in bfloat16 or wider, within the bound.
No kernel may reach another device: no remote copies, remote signals or barrier semaphores. Data moves between devices by JAX's collectives and lax.ppermute only.
A program may use at most 192 MiB of HBM per device.

v0:
```python
import jax
import jax.numpy as jnp
from jax import lax
from jax.sharding import PartitionSpec as P

HEADS = 16
HEAD_DIM = 64
FF = 4096
QBLOCK = 512
STEP = 10
LONGEST = 1024


eps_norm = 1e-05
beta_one = 0.9
beta_two = 0.999
eps_adam = 1e-08
rate_matrix = 0.02
rate_vector = 0.2
decay_matrix = 0.1
blocked = -1e30


def norm_forward(values, gain, bias):
    mean_row = jnp.mean(values, -1, keepdims=True)
    centred = values - mean_row
    spread = jnp.mean(centred * centred, -1, keepdims=True)
    scale_row = lax.rsqrt(spread + eps_norm)
    normal = centred * scale_row
    return (normal * gain + bias, normal, scale_row)


def norm_backward(grad_out, normal, scale_row, gain):
    grad_normal = grad_out * gain
    first_term = jnp.mean(grad_normal, -1, keepdims=True)
    second_term = jnp.mean(grad_normal * normal, -1, keepdims=True)
    grad_in = scale_row * (grad_normal - first_term - normal * second_term)
    return (grad_in, jnp.sum(grad_out * normal, 0), jnp.sum(grad_out, 0))


def gelu_exact(values):
    return jax.nn.gelu(values, approximate=False)


def contract_rows(left, right):
    return lax.dot_general(
        left, right, (((0,), (0,)), ((), ())), preferred_element_type=jnp.float32
    )


def contract_cols(left, right):
    return lax.dot_general(
        left, right, (((1,), (1,)), ((), ())), preferred_element_type=jnp.float32
    )


def block_mask(start, segment_ids, segment_pad):
    query_pos = start + jnp.arange(QBLOCK, dtype=jnp.int32)
    key_pos = start - LONGEST + jnp.arange(LONGEST + QBLOCK, dtype=jnp.int32)
    query_seg = lax.dynamic_slice_in_dim(segment_ids, start, QBLOCK, 0)
    key_seg = lax.dynamic_slice_in_dim(segment_pad, start, LONGEST + QBLOCK, 0)
    return (key_pos[None, :] <= query_pos[:, None]) & (key_seg[None, :] == query_seg[:, None])


def block_scores(queries, keys_pad, start, segment_ids, segment_pad):
    query_block = lax.dynamic_slice_in_dim(queries, start, QBLOCK, 0)
    key_block = lax.dynamic_slice_in_dim(keys_pad, start, LONGEST + QBLOCK, 0)
    scores = jnp.einsum(
        "qhd,khd->hqk", query_block, key_block, preferred_element_type=jnp.float32
    ) * HEAD_DIM ** (-0.5)
    valid = block_mask(start, segment_ids, segment_pad)
    return (jnp.where(valid[None], scores, blocked), query_block, key_block)


def attend_forward(queries, keys_pad, values_pad, segment_ids, segment_pad):
    blocks = queries.shape[0] // QBLOCK

    def one_block(index):
        start = index * QBLOCK
        scores, query_block, key_block = block_scores(
            queries, keys_pad, start, segment_ids, segment_pad
        )
        value_block = lax.dynamic_slice_in_dim(values_pad, start, LONGEST + QBLOCK, 0)
        peak = jnp.max(scores, 2, keepdims=True)
        raised = jnp.exp(scores - peak)
        total = jnp.sum(raised, 2, keepdims=True)
        shares_low = (raised / total).astype(jnp.bfloat16)
        result = jnp.einsum(
            "hqk,khd->qhd", shares_low, value_block, preferred_element_type=jnp.float32
        )
        return (result, (peak + jnp.log(total))[:, :, 0])

    results, log_total = lax.map(one_block, jnp.arange(blocks, dtype=jnp.int32))
    return (results.reshape(queries.shape[0], queries.shape[1], queries.shape[2]), log_total)


def attend_backward(
    queries, keys_pad, values_pad, grad_attended, log_total, segment_ids, segment_pad
):
    blocks = queries.shape[0] // QBLOCK
    width = LONGEST + QBLOCK
    scale = HEAD_DIM ** (-0.5)

    def one_block(carry, inputs):
        grad_keys, grad_values = carry
        index, block_total = inputs
        start = index * QBLOCK
        scores, query_block, key_block = block_scores(
            queries, keys_pad, start, segment_ids, segment_pad
        )
        value_block = lax.dynamic_slice_in_dim(values_pad, start, width, 0)
        grad_block = lax.dynamic_slice_in_dim(grad_attended, start, QBLOCK, 0)
        shares = jnp.exp(scores - block_total[:, :, None])
        grad_shares = jnp.einsum(
            "qhd,khd->hqk", grad_block, value_block, preferred_element_type=jnp.float32
        )
        delta = jnp.sum(shares * grad_shares, 2, keepdims=True)
        grad_scores = (shares * (grad_shares - delta)).astype(jnp.bfloat16)
        grad_query = (
            jnp.einsum("hqk,khd->qhd", grad_scores, key_block, preferred_element_type=jnp.float32)
            * scale
        )
        grad_key = (
            jnp.einsum("hqk,qhd->khd", grad_scores, query_block, preferred_element_type=jnp.float32)
            * scale
        )
        grad_value = jnp.einsum(
            "hqk,qhd->khd",
            shares.astype(jnp.bfloat16),
            grad_block,
            preferred_element_type=jnp.float32,
        )
        grad_keys = lax.dynamic_update_slice_in_dim(
            grad_keys, lax.dynamic_slice_in_dim(grad_keys, start, width, 0) + grad_key, start, 0
        )
        grad_values = lax.dynamic_update_slice_in_dim(
            grad_values,
            lax.dynamic_slice_in_dim(grad_values, start, width, 0) + grad_value,
            start,
            0,
        )
        return ((grad_keys, grad_values), grad_query)

    zero_pad = jnp.zeros(keys_pad.shape, jnp.float32)
    (grad_keys, grad_values), grad_queries = lax.scan(
        one_block, (zero_pad, zero_pad), (jnp.arange(blocks, dtype=jnp.int32), log_total)
    )
    grad_queries = grad_queries.reshape(queries.shape[0], queries.shape[1], queries.shape[2])
    return (grad_queries, grad_keys[LONGEST:], grad_values[LONGEST:])


def adam_update(master, first, second, grad, rate, decay):
    moment = beta_one * first + (1.0 - beta_one) * grad
    square = beta_two * second + (1.0 - beta_two) * grad * grad
    step_size = (
        moment / (1.0 - beta_one**STEP) / (jnp.sqrt(square / (1.0 - beta_two**STEP)) + eps_adam)
    )
    updated = master - rate * (step_size + decay * master)
    return (updated, moment, square)


def body(
    tokens,
    out_grad,
    seq_lengths,
    master_qkv,
    first_qkv,
    second_qkv,
    master_mix,
    first_mix,
    second_mix,
    master_up,
    first_up,
    second_up,
    master_down,
    first_down,
    second_down,
    master_norms,
    first_norms,
    second_norms,
    master_midnorm,
    first_midnorm,
    second_midnorm,
    master_heads,
    first_heads,
    second_heads,
):
    parts = lax.axis_size("tensor")
    place = lax.axis_index("tensor")
    qkv_full, mix_full, up_full, down_full = (
        lax.all_gather(master_qkv.astype(jnp.bfloat16), "dp", axis=0, tiled=True),
        lax.all_gather(master_mix.astype(jnp.bfloat16), "dp", axis=0, tiled=True),
        lax.all_gather(master_up.astype(jnp.bfloat16), "dp", axis=0, tiled=True),
        lax.all_gather(master_down.astype(jnp.bfloat16), "dp", axis=0, tiled=True),
    )
    rows_local = tokens.shape[0]
    model = tokens.shape[1]
    group_rows = rows_local * parts
    heads_local = mix_full.shape[1] // HEAD_DIM
    width_local = up_full.shape[1]
    qkv_matrix = qkv_full.reshape(model, 3 * heads_local * HEAD_DIM)
    ends = jnp.cumsum(seq_lengths[0])
    places = jnp.arange(group_rows, dtype=jnp.int32)
    segment_ids = jnp.sum((places[:, None] >= ends[None, :]).astype(jnp.int32), 1)
    segment_pad = jnp.concatenate([jnp.full((LONGEST,), -1, jnp.int32), segment_ids], 0)
    inputs = tokens.astype(jnp.float32)
    normed_one, normal_one, scale_one = norm_forward(inputs, master_norms[0], master_norms[1])
    gathered_one = lax.all_gather(normed_one.astype(jnp.bfloat16), "tensor", axis=0, tiled=True)
    packed = jnp.dot(gathered_one, qkv_matrix, preferred_element_type=jnp.float32).astype(
        jnp.bfloat16
    )
    packed = packed.reshape(group_rows, 3, heads_local, HEAD_DIM)
    queries = packed[:, 0]
    padding = jnp.zeros((LONGEST, heads_local, HEAD_DIM), jnp.bfloat16)
    keys_pad = jnp.concatenate([padding, packed[:, 1]], 0)
    values_pad = jnp.concatenate([padding, packed[:, 2]], 0)
    attended, log_total = attend_forward(queries, keys_pad, values_pad, segment_ids, segment_pad)
    head_gain = lax.dynamic_slice_in_dim(master_heads, place * heads_local, heads_local, 0)
    scaled = (
        (attended * head_gain[None, :, None])
        .astype(jnp.bfloat16)
        .reshape(group_rows, heads_local * HEAD_DIM)
    )
    mixed = lax.psum_scatter(
        contract_cols(scaled, mix_full), "tensor", scatter_dimension=0, tiled=True
    )
    post, normal_two, scale_two = norm_forward(mixed, master_norms[2], master_norms[3])
    hidden = inputs + post
    normed_three, normal_three, scale_three = norm_forward(hidden, master_norms[4], master_norms[5])
    normed_low = normed_three.astype(jnp.bfloat16)
    mid_local = lax.dynamic_slice_in_dim(master_midnorm, place * width_local, width_local, 1)
    gathered_two = lax.all_gather(normed_low, "tensor", axis=0, tiled=True)
    upper = jnp.dot(gathered_two, up_full, preferred_element_type=jnp.float32)
    activated, gelu_back = jax.vjp(gelu_exact, upper)
    total_one, total_two = lax.psum(
        (jnp.sum(activated, 1), jnp.sum(activated * activated, 1)), "tensor"
    )
    mean_row = total_one[:, None] / FF
    scale_mid = lax.rsqrt(total_two[:, None] / FF - mean_row * mean_row + eps_norm)
    normal_mid = (activated - mean_row) * scale_mid
    reshaped = (normal_mid * mid_local[0] + mid_local[1]).astype(jnp.bfloat16)
    output_ffn = lax.psum_scatter(
        contract_cols(reshaped, down_full), "tensor", scatter_dimension=0, tiled=True
    )
    piece = lax.all_gather(out_grad, "tensor", axis=0, tiled=True)
    grad_buffer = jnp.dot(piece, down_full, preferred_element_type=jnp.float32)
    rows = reshaped
    grad_reshaped = grad_buffer
    grad_down = contract_rows(piece, rows)
    grad_normal_mid = grad_reshaped * mid_local[0]
    sum_one, sum_two = lax.psum(
        (jnp.sum(grad_normal_mid, 1), jnp.sum(grad_normal_mid * normal_mid, 1)), "tensor"
    )
    grad_activated = scale_mid * (
        grad_normal_mid - sum_one[:, None] / FF - normal_mid * (sum_two[:, None] / FF)
    )
    grad_upper = gelu_back(grad_activated)[0].astype(jnp.bfloat16)
    grad_mid_local = jnp.stack([jnp.sum(grad_reshaped * normal_mid, 0), jnp.sum(grad_reshaped, 0)])
    grad_midnorm_part = lax.dynamic_update_slice_in_dim(
        jnp.zeros((2, FF), jnp.float32), grad_mid_local, place * width_local, 1
    )
    grad_up = contract_rows(gathered_two, grad_upper)
    grad_normed_three = lax.psum_scatter(
        contract_cols(grad_upper, up_full), "tensor", scatter_dimension=0, tiled=True
    )
    layer_out = (hidden + output_ffn).astype(jnp.bfloat16)
    grad_hidden_ffn, grad_gain_three, grad_bias_three = norm_backward(
        grad_normed_three, normal_three, scale_three, master_norms[4]
    )
    grad_hidden = out_grad.astype(jnp.float32) + grad_hidden_ffn
    grad_mixed, grad_gain_two, grad_bias_two = norm_backward(
        grad_hidden, normal_two, scale_two, master_norms[2]
    )
    piece = lax.all_gather(grad_mixed.astype(jnp.bfloat16), "tensor", axis=0, tiled=True)
    grad_buffer = jnp.dot(piece, mix_full, preferred_element_type=jnp.float32)
    rows = scaled
    grad_scaled = grad_buffer
    grad_mix = contract_rows(piece, rows)
    grad_scaled = grad_scaled.reshape(group_rows, heads_local, HEAD_DIM)
    grad_head_local = jnp.sum(grad_scaled * attended, (0, 2))
    grad_heads_part = lax.dynamic_update_slice_in_dim(
        jnp.zeros((HEADS,), jnp.float32), grad_head_local, place * heads_local, 0
    )
    grad_attended = (grad_scaled * head_gain[None, :, None]).astype(jnp.bfloat16)
    grad_queries, grad_keys, grad_values = attend_backward(
        queries, keys_pad, values_pad, grad_attended, log_total, segment_ids, segment_pad
    )
    grad_packed = (
        jnp.stack([grad_queries, grad_keys, grad_values], 1)
        .astype(jnp.bfloat16)
        .reshape(group_rows, 3 * heads_local * HEAD_DIM)
    )
    grad_qkv = contract_rows(gathered_one, grad_packed).reshape(model, 3, heads_local * HEAD_DIM)
    grad_normed_one = lax.psum_scatter(
        contract_cols(grad_packed, qkv_matrix), "tensor", scatter_dimension=0, tiled=True
    )
    grad_in, grad_gain_one, grad_bias_one = norm_backward(
        grad_normed_one, normal_one, scale_one, master_norms[0]
    )
    input_grad = grad_hidden + grad_in
    shard_qkv, shard_mix, shard_up, shard_down = (
        lax.psum_scatter(grad_qkv, "dp", scatter_dimension=0, tiled=True),
        lax.psum_scatter(grad_mix, "dp", scatter_dimension=0, tiled=True),
        lax.psum_scatter(grad_up, "dp", scatter_dimension=0, tiled=True),
        lax.psum_scatter(grad_down, "dp", scatter_dimension=0, tiled=True),
    )
    grad_norms_part = jnp.stack(
        [
            grad_gain_one,
            grad_bias_one,
            grad_gain_two,
            grad_bias_two,
            grad_gain_three,
            grad_bias_three,
        ]
    )
    grad_norms, grad_midnorm, grad_heads = lax.psum(
        (grad_norms_part, grad_midnorm_part, grad_heads_part), ("dp", "tensor")
    )
    new_qkv = adam_update(master_qkv, first_qkv, second_qkv, shard_qkv, rate_matrix, decay_matrix)
    new_mix = adam_update(master_mix, first_mix, second_mix, shard_mix, rate_matrix, decay_matrix)
    new_up = adam_update(master_up, first_up, second_up, shard_up, rate_matrix, decay_matrix)
    new_down = adam_update(
        master_down, first_down, second_down, shard_down, rate_matrix, decay_matrix
    )
    new_norms = adam_update(master_norms, first_norms, second_norms, grad_norms, rate_vector, 0.0)
    new_midnorm = adam_update(
        master_midnorm, first_midnorm, second_midnorm, grad_midnorm, rate_vector, 0.0
    )
    new_heads = adam_update(master_heads, first_heads, second_heads, grad_heads, rate_vector, 0.0)
    return (
        layer_out,
        input_grad,
        new_qkv[0],
        new_qkv[1],
        new_qkv[2],
        new_mix[0],
        new_mix[1],
        new_mix[2],
        new_up[0],
        new_up[1],
        new_up[2],
        new_down[0],
        new_down[1],
        new_down[2],
        new_norms[0],
        new_norms[1],
        new_norms[2],
        new_midnorm[0],
        new_midnorm[1],
        new_midnorm[2],
        new_heads[0],
        new_heads[1],
        new_heads[2],
    )


def solution(mesh):
    in_specs = (
        P(("dp", "tensor"), None),
        P(("dp", "tensor"), None),
        P("dp", None),
        P("dp", None, "tensor"),
        P("dp", None, "tensor"),
        P("dp", None, "tensor"),
        P("dp", "tensor"),
        P("dp", "tensor"),
        P("dp", "tensor"),
        P("dp", "tensor"),
        P("dp", "tensor"),
        P("dp", "tensor"),
        P("dp", "tensor"),
        P("dp", "tensor"),
        P("dp", "tensor"),
        P(),
        P(),
        P(),
        P(),
        P(),
        P(),
        P(),
        P(),
        P(),
    )
    out_specs = (
        P(("dp", "tensor"), None),
        P(("dp", "tensor"), None),
        P("dp", None, "tensor"),
        P("dp", None, "tensor"),
        P("dp", None, "tensor"),
        P("dp", "tensor"),
        P("dp", "tensor"),
        P("dp", "tensor"),
        P("dp", "tensor"),
        P("dp", "tensor"),
        P("dp", "tensor"),
        P("dp", "tensor"),
        P("dp", "tensor"),
        P("dp", "tensor"),
        P(),
        P(),
        P(),
        P(),
        P(),
        P(),
        P(),
        P(),
        P(),
    )
    return jax.shard_map(body, mesh=mesh, in_specs=in_specs, out_specs=out_specs, check_vma=False)
```

profile of v0, /device:TPU:0, one launch (start us, length us, event | category | flops | bytes accessed | tf_op | source)
XLA Modules:
  0.0 1578.6 jit_solution(1874254268514845607)
XLA Ops:
  18.3 12.9 all_gather.26
  31.2 8.6 all-gather.10.cloned.1.call-done
  39.8 82.9 %all-gather.8.cloned.1.call-done = bf16[2048,1024]{1,0:T(8,128)(2,1)} async-done(((bf16[512,1024]{1,0:T(8,128)(2,1)}), bf16[2048,1024]{1,0:T(8,128)(2,1)}) %all-gather.8.cloned.1.call-update) | async-done | bytes 4194320 | tf_op jit(solution)/shard_map/all_gather | solution.py:208
  122.8 6.1 convolution_convert_fusion
  130.7 98.1 %while.32 = (s32[]{:T(128)}, f32[4,512,4,64]{1,0,3,2:T(4,128)}, f32[4,4,512]{2,1,0:T(4,128)}, s32[4]{0:T(128)S(1)}, bf16[3072,4,64]{0,2,1:T(8,128)(2,1)}, /*inde...) while((s32[]{:T(128)}, f32[4,512,4,64]{1,0,3,2:T(4,128)}, ...), condition=%wide.region_7.8_spmd.clone, body=%wide.region_4.7_spmd.sunk.clone | while | flops 845414400 | bytes 51749632 | solution.py:93
  144.3 11.1 dynamic_update_slice.55
  168.8 11.1 dynamic_update_slice.55
  193.2 11.1 dynamic_update_slice.55
  217.7 11.1 dynamic_update_slice.55
  241.9 139.5 %reduce-scatter.9.cloned.1.call-done = f32[512,1024]{1,0:T(8,128)} async-done(((f32[2048,1024]{1,0:T(8,128)}), f32[512,1024]{1,0:T(8,128)}) %reduce-scatter.9.cloned.1.call-update) | async-done | bytes 2097168 | tf_op jit(solution)/shard_map/reduce_scatter | solution.py:224
  390.2 22.2 %all-gather.16.cloned.1.call-done = bf16[1024,1024]{1,0:T(8,128)(2,1)} async-done(((bf16[128,1024]{1,0:T(8,128)(2,1)}), bf16[1024,1024]{1,0:T(8,128)(2,1)}) %all-gather.16.cloned.1.call-update) | async-done | bytes 2097168 | tf_op jit(solution)/shard_map/all_gather | solution.py:194
  412.4 82.2 %all-gather.18.cloned.1.call-done = bf16[2048,1024]{1,0:T(8,128)(2,1)} async-done(((bf16[512,1024]{1,0:T(8,128)(2,1)}), bf16[2048,1024]{1,0:T(8,128)(2,1)}) %all-gather.18.cloned.1.call-update) | async-done | bytes 4194320 | tf_op jit(solution)/shard_map/all_gather | solution.py:245
  494.6 11.2 fusion.82
  505.8 9.3 copy.61
  515.1 8.3 all-gather.14.cloned.1.call-done
  523.4 82.9 %all-gather.12.cloned.1.call-done = bf16[2048,1024]{1,0:T(8,128)(2,1)} async-done(((bf16[512,1024]{1,0:T(8,128)(2,1)}), bf16[2048,1024]{1,0:T(8,128)(2,1)}) %all-gather.12.cloned.1.call-update) | async-done | bytes 4194320 | tf_op jit(solution)/shard_map/all_gather | solution.py:232
  606.3 27.1 %fusion.71 = (f32[2048]{0:T(1024)S(1)}, f32[2048]{0:T(1024)S(1)}, f32[2048,1024]{0,1:T(8,128)}, f32[2048,1024]{0,1:T(8,128)}, f32[2048,1024]{0,1:T(8,128)}) fusion(bf16[2048,1024]{1,0:T(8,128)(2,1)} %all-gather.12.cloned.1.call-done, bf16[1024,1024]{1,0:T(8,128)(2,1)} %all-gather.14.cloned.1.call-done), kind=kOutput, calls=%fused_computation.168 | convolution fusion | flops 4435472384 | bytes 31473664 | tf_op jit(solution)/shard_map/dot_general | solution.py:233
  633.4 16.3 %all-reduce.5 = (f32[2048]{0:T(1024)S(1)}, f32[2048]{0:T(1024)S(1)}) all-reduce(f32[2048]{0:T(1024)S(1)} %get-tuple-element.297, f32[2048]{0:T(1024)S(1)} %get-tuple-element.296), channel_id=1, replica_groups=mesh['dp'=8,'tensor'=4] {'tensor'}, use_global_device_ids=true, to_apply=%region_16.17 | all-reduce | flops 4096 | bytes 32768 | tf_op jit(solution)/shard_map/psum | solution.py:235
  649.7 7.9 multiply_reduce_fusion.1
  657.7 15.8 %all-reduce.4 = (f32[2048]{0:T(1024)S(1)}, f32[2048]{0:T(1024)S(1)}) all-reduce(f32[2048]{0:T(1024)S(1)} %get-tuple-element.294, f32[2048]{0:T(1024)S(1)} %get-tuple-element.295), channel_id=1, replica_groups=mesh['dp'=8,'tensor'=4] {'tensor'}, use_global_device_ids=true, to_apply=%region_21.22 | all-reduce | flops 4096 | bytes 32768 | tf_op jit(solution)/shard_map/psum | solution.py:251
  673.5 15.4 add_convert_fusion
  690.9 6.8 fusion.84
  697.8 10.7 fusion.83
  708.9 131.8 %reduce-scatter.13.cloned.1.call-done = f32[512,1024]{1,0:T(8,128)} async-done(((f32[2048,1024]{1,0:T(8,128)}), f32[512,1024]{1,0:T(8,128)}) %reduce-scatter.13.cloned.1.call-update) | async-done | bytes 2097168 | tf_op jit(solution)/shard_map/reduce_scatter | solution.py:263
  843.8 144.5 %reduce-scatter.11.cloned.1.call-done = f32[512,1024]{1,0:T(8,128)} async-done(((f32[2048,1024]{1,0:T(8,128)}), f32[512,1024]{1,0:T(8,128)}) %reduce-scatter.11.cloned.1.call-update) | async-done | bytes 2097168 | tf_op jit(solution)/shard_map/reduce_scatter | solution.py:242
  988.4 5.4 multiply_reduce_fusion.7
  996.7 10.0 fusion.86
  1008.1 10.0 convolution_bitcast_fusion
  1018.1 60.2 %all-gather.20.cloned.1.call-done = bf16[2048,1024]{1,0:T(8,128)(2,1)} async-done(((bf16[512,1024]{1,0:T(8,128)(2,1)}), bf16[2048,1024]{1,0:T(8,128)(2,1)}) %all-gather.20.cloned.1.call-update) | async-done | bytes 4194320 | tf_op jit(solution)/shard_map/all_gather | solution.py:274
  1086.8 192.0 %while.33 = (s32[]{:T(128)}, f32[3072,4,64]{0,2,1:T(8,128)}, f32[3072,4,64]{0,2,1:T(8,128)}, bf16[4,512,4,64]{1,0,3,2:T(4,128)(2,1)}, s32[4]{0:T(128)S(1)}, /*in...) while((s32[]{:T(128)}, f32[3072,4,64]{0,2,1:T(8,128)}, ...), condition=%wide.region_29.30_spmd.clone, body=%wide.region_27.29_spmd.sunk.clone | while | flops 2045378560 | bytes 268517984 | solution.py:145
  1088.3 7.8 fusion.154
  1099.2 8.2 multiply_reduce_fusion.17
  1127.4 8.0 fusion.156
  1136.8 8.3 fusion.154
  1148.3 8.0 multiply_reduce_fusion.17
  1176.3 8.2 fusion.156
  1185.8 7.5 fusion.154
  1196.5 7.9 multiply_reduce_fusion.17
  1223.7 7.9 fusion.156
  1233.0 7.4 fusion.154
  1243.7 7.9 multiply_reduce_fusion.17
  1270.9 7.9 fusion.156
  1280.7 5.3 fusion.69
  1297.2 7.7 fusion.85
  1316.0 6.7 reduce-scatter.19.cloned.1.call-done
  1324.5 47.6 %reduce-scatter.17.cloned.1.call-done = f32[128,3,256]{2,0,1:T(8,128)} async-done(((f32[1024,3,256]{2,0,1:T(8,128)}), f32[128,3,256]{2,0,1:T(8,128)}) %reduce-scatter.17.cloned.1.call-update) | async-done | bytes 393232 | tf_op jit(solution)/shard_map/reduce_scatter | solution.py:302
  1374.6 144.4 %reduce-scatter.15.cloned.1.call-done = f32[512,1024]{1,0:T(8,128)} async-done(((f32[2048,1024]{1,0:T(8,128)}), f32[512,1024]{1,0:T(8,128)}) %reduce-scatter.15.cloned.1.call-update) | async-done | bytes 2097168 | tf_op jit(solution)/shard_map/reduce_scatter | solution.py:294
  1522.2 41.8 %all-reduce.3 = (f32[6,1024]{1,0:T(8,128)S(1)}, f32[2,4096]{1,0:T(2,128)S(1)}, f32[16]{0:T(128)S(1)}) all-reduce(f32[6,1024]{1,0:T(8,128)S(1)} %stack.48, f32[2,4096]{1,0:T(2,128)} %maximum_dynamic-update-slice_fusion, f32[16]{0:T(128)} %dynamic_update_slice.39), channel_id=1, replica_groups=mesh['dp'=8,'tensor'=4] {'dp','tensor'}, use_global_device_ids=true, to_apply=%region_43.44 | all-reduce | flops 14352 | bytes 114816 | tf_op jit(solution)/shard_map/psum | solution.py:317
  (397 shorter events, 236.6 us)
Async XLA Ops:
  7.2 10.0 copy-start.56
  7.2 10.2 copy-start.52
  7.2 11.0 copy-start.35
  7.2 32.6 %all-gather.10.cloned.1.call-start = ((), (), s32[]{:S(2)}) async-start(), calls=%async_computation.9 | async-start | bytes 1769472 | tf_op jit(solution)/shard_map/all_gather | solution.py:191
  9.1 113.6 %all-gather.8.cloned.1.call-start = ((), (), s32[]{:S(2)}) async-start(), calls=%async_computation.8 | async-start | bytes 5242880 | tf_op jit(solution)/shard_map/all_gather | solution.py:208
  17.2 364.3 %reduce-scatter.9.cloned.1.call-start = ((), (), s32[]{:S(2)}) async-start(), calls=%async_computation.10 | async-start | bytes 10485760 | tf_op jit(solution)/shard_map/reduce_scatter | solution.py:224
  18.2 214.1 %copy-start.47 = (f32[256]{0:T(256)}, f32[256]{0:T(256)S(1)}, u32[]{:S(2)}) copy-start(f32[256]{0:T(256)S(1)} %mul.527) | copy-start | bytes 3076
  228.8 9.4 copy-start.2
  228.8 9.4 copy-start.11
  228.8 9.4 copy-start.29
  228.8 9.4 copy-start.36
  238.3 146.9 %copy-start.9 = (bf16[512,1024]{1,0:T(8,128)(2,1)S(1)}, bf16[512,1024]{1,0:T(8,128)(2,1)}, u32[]{:S(2)}) copy-start(bf16[512,1024]{1,0:T(8,128)(2,1)} %param.28) | copy-start | bytes 3145732
  238.3 174.1 %all-gather.16.cloned.1.call-start = ((), (), s32[]{:S(2)}) async-start(), calls=%async_computation.13 | async-start | bytes 2359296 | tf_op jit(solution)/shard_map/all_gather | solution.py:194
  240.0 254.6 %all-gather.18.cloned.1.call-start = ((), (), s32[]{:S(2)}) async-start(), calls=%async_computation.15 | async-start | bytes 5242880 | tf_op jit(solution)/shard_map/all_gather | solution.py:245
  240.6 282.8 %all-gather.14.cloned.1.call-start = ((), (), s32[]{:S(2)}) async-start(), calls=%async_computation.12 | async-start | bytes 2359296 | tf_op jit(solution)/shard_map/all_gather | solution.py:193
  241.4 364.9 %all-gather.12.cloned.1.call-start = ((), (), s32[]{:S(2)}) async-start(), calls=%async_computation.11 | async-start | bytes 5242880 | tf_op jit(solution)/shard_map/all_gather | solution.py:232
  389.3 451.5 %reduce-scatter.13.cloned.1.call-start = ((), (), s32[]{:S(2)}) async-start(), calls=%async_computation.16 | async-start | bytes 10485760 | tf_op jit(solution)/shard_map/reduce_scatter | solution.py:263
  673.5 17.4 %copy-start.54 = (bf16[1024,1024]{1,0:T(8,128)(2,1)S(1)}, bf16[1024,1024]{1,0:T(8,128)(2,1)}, u32[]{:S(2)}) copy-start(bf16[1024,1024]{1,0:T(8,128)(2,1)} %all-gather.14.cloned.1.call-done) | copy-start | bytes 6291460
  697.7 290.7 %reduce-scatter.11.cloned.1.call-start = ((), (), s32[]{:S(2)}) async-start(), calls=%async_computation.14 | async-start | bytes 10485760 | tf_op jit(solution)/shard_map/reduce_scatter | solution.py:242
  708.5 279.9 %copy-start.20 = (bf16[512,1024]{1,0:T(8,128)(2,1)S(1)}, bf16[512,1024]{1,0:T(8,128)(2,1)}, u32[]{:S(2)}) copy-start(bf16[512,1024]{1,0:T(8,128)(2,1)} %param.29) | copy-start | bytes 3145732
  708.5 369.8 %all-gather.20.cloned.1.call-start = ((), (), s32[]{:S(2)}) async-start(), calls=%async_computation.17 | async-start | bytes 5242880 | tf_op jit(solution)/shard_map/all_gather | solution.py:274
  996.7 309.6 %reduce-scatter.21.cloned.1.call-start = ((), (), s32[]{:S(2)}) async-start(), calls=%async_computation.21 | async-start | bytes 4718592 | tf_op jit(solution)/shard_map/reduce_scatter | solution.py:304
  1006.7 302.1 %reduce-scatter.23.cloned.1.call-start = ((), (), s32[]{:S(2)}) async-start(), calls=%async_computation.22 | async-start | bytes 4718592 | tf_op jit(solution)/shard_map/reduce_scatter | solution.py:305
  1018.0 60.3 %copy-start.8 = (f32[32,8,4,512]{3,1,2,0:T(8,128)S(1)}, f32[32,8,4,512]{3,1,2,0:T(8,128)}, u32[]{:S(2)}) copy-start(f32[32,8,4,512]{3,1,2,0:T(8,128)} %copy-done.7) | copy-start | bytes 6291460
  1018.0 60.3 %copy-start.18 = (bf16[1024,256]{1,0:T(8,128)(2,1)S(1)}, bf16[1024,256]{1,0:T(8,128)(2,1)}, u32[]{:S(2)}) copy-start(bf16[1024,256]{1,0:T(8,128)(2,1)} %all_gather.26) | copy-start | bytes 1572868
  1018.0 64.4 %copy-start.51 = (f32[4]{0:T(128)S(1)}, f32[4]{0:T(128)}, u32[]{:S(2)}) copy-start(f32[4]{0:T(128)} %copy-done.50) | copy-start | bytes 52
  1018.0 304.6 %reduce-scatter.19.cloned.1.call-start = ((), (), s32[]{:S(2)}) async-start(), calls=%async_computation.20 | async-start | bytes 1179648 | tf_op jit(solution)/shard_map/reduce_scatter | solution.py:303
  1086.8 193.8 %copy-start.48 = (f32[256]{0:T(256)S(1)}, f32[256]{0:T(256)}, u32[]{:S(2)}) copy-start(f32[256]{0:T(256)} %copy-done.47) | copy-start | bytes 3076
  1087.0 9.1 copy-start.15
  1099.2 8.3 slice-start
  1099.2 8.3 slice-start.1
  1099.2 10.1 slice-start.2
  1135.4 9.7 copy-start.15
  1148.3 8.9 slice-start.2
  1176.3 8.2 copy-start.22
  1184.5 8.8 copy-start.15
  1196.5 8.8 slice-start.2
  1231.7 8.8 copy-start.15
  1243.7 8.8 slice-start.2
  1287.7 84.5 %reduce-scatter.17.cloned.1.call-start = ((), (), s32[]{:S(2)}) async-start(), calls=%async_computation.19 | async-start | bytes 3538944 | tf_op jit(solution)/shard_map/reduce_scatter | solution.py:302
  1297.2 221.8 %reduce-scatter.15.cloned.1.call-start = ((), (), s32[]{:S(2)}) async-start(), calls=%async_computation.18 | async-start | bytes 10485760 | tf_op jit(solution)/shard_map/reduce_scatter | solution.py:294
  1305.0 67.2 %copy-start.28 = (f32[128,3,256]{2,0,1:T(8,128)S(1)}, f32[128,3,256]{2,0,1:T(8,128)}, u32[]{:S(2)}) copy-start(f32[128,3,256]{2,0,1:T(8,128)} %param.31) | copy-start | bytes 1179652
  1308.8 210.2 %copy-start.10 = (bf16[512,1024]{1,0:T(8,128)(2,1)S(1)}, bf16[512,1024]{1,0:T(8,128)(2,1)}, u32[]{:S(2)}) copy-start(bf16[512,1024]{1,0:T(8,128)(2,1)} %param.28) | copy-start | bytes 3145732
  1308.8 210.2 %copy-start.38 = (f32[1,1024]{1,0:T(1,128)S(1)}, f32[1,1024]{1,0:T(1,128)}, u32[]{:S(2)}) copy-start(f32[1,1024]{1,0:T(1,128)} %copy-done.37) | copy-start | bytes 12292
  1308.8 210.2 %copy-start.41 = (f32[512]{0:T(512)S(1)}, f32[512]{0:T(512)}, u32[]{:S(2)}) copy-start(f32[512]{0:T(512)} %copy-done.40) | copy-start | bytes 6148
  1308.8 210.2 %copy-start.43 = (f32[512]{0:T(512)S(1)}, f32[512]{0:T(512)}, u32[]{:S(2)}) copy-start(f32[512]{0:T(512)} %copy-done.42) | copy-start | bytes 6148
  1311.4 210.1 %copy-start.44 = (f32[1024]{0:T(1024)S(1)}, f32[1024]{0:T(1024)}, u32[]{:S(2)}) copy-start(f32[1024]{0:T(1024)} %get-tuple-element.298) | copy-start | bytes 12292
  1311.4 256.8 %copy-start.14 = (f32[512,1024]{1,0:T(8,128)S(1)}, f32[512,1024]{1,0:T(8,128)}, u32[]{:S(2)}) copy-start(f32[512,1024]{1,0:T(8,128)} %copy-done.13) | copy-start | bytes 6291460
  (66 other events, 304.7 us)
Sparse Core Ops, SparseCore 0:
  10.5 29.2 all-gather.9
  42.0 80.7 all-gather.7
  238.4 143.0 reduce-scatter.8
  383.7 28.5 all-gather.15
  413.8 80.7 all-gather.17
  496.9 26.4 all-gather.13
  525.5 80.7 all-gather.11
  697.8 142.8 reduce-scatter.12
  843.1 145.1 reduce-scatter.10
  996.8 81.4 all-gather.19
  1081.7 49.8 reduce-scatter.20
  1135.2 51.2 reduce-scatter.22
  1287.8 34.8 reduce-scatter.18
  1325.9 46.2 reduce-scatter.16
  1374.5 144.4 reduce-scatter.14
where the time goes:
time: 1590 us; the launch traced here: 1580 us
  waiting for transfers between devices  963 us (61%)
  matrix products  256 us (16%)
  local copies, waits for them, and re-layouts  138 us (9%)
  other arithmetic  113 us (7%)
  blocking collectives  86.8 us (5%)
    reduce_scatter x1, waiting for transfers between devices, body(): lax.psum_scatter(contract_cols(reshaped, down_full), 'tensor', scatter_di...  145 us
    reduce_scatter x1, waiting for transfers between devices, body(): lax.psum_scatter(contract_cols(grad_packed, qkv_matrix), 'tensor', scatte...  144 us
    reduce_scatter x1, waiting for transfers between devices, body(): lax.psum_scatter(contract_cols(scaled, mix_full), 'tensor', scatter_dimen...  140 us
    reduce_scatter x1, waiting for transfers between devices, body(): lax.psum_scatter(contract_cols(grad_upper, up_full), 'tensor', scatter_di...  132 us
    all_gather x1, waiting for transfers between devices, body(): lax.all_gather(normed_one.astype(jnp.bfloat16), 'tensor', axis=0, tiled=T...  82.9 us
    all_gather x1, waiting for transfers between devices, body(): gathered_two = lax.all_gather(normed_low, 'tensor', axis=0, tiled=True)  82.9 us
    all_gather x1, waiting for transfers between devices, body(): piece = lax.all_gather(out_grad, 'tensor', axis=0, tiled=True)  82.2 us
    dynamic_update_slice x16, local copies, waits for them, and re-layouts, attend_forward(): results, log_total = lax.map(one_block, jnp.arange(blocks, dtype=jnp.int32))  66.5 us
  transfers between devices with their start and end apart: 15, of which 13 were waited for; matrix products, arithmetic and copies ran while one was open for 18% of the time, Pallas kernels for 0%

commit v1 on v0

v1 whole, which is shorter than its diff:
```python
import functools
import math

import jax
import jax.numpy as jnp
from jax import lax
from jax.experimental import pallas as pl
from jax.experimental.pallas import tpu as pltpu
from jax.sharding import PartitionSpec as P

HEADS = 16
HEAD_DIM = 64
FF = 4096
STEP = 10
LONGEST = 1024

eps_norm = 1e-05
beta_one = 0.9
beta_two = 0.999
eps_adam = 1e-08
rate_matrix = 0.02
rate_vector = 0.2
decay_matrix = 0.1
blocked = -1e30

KEYS = 256
BF = jnp.bfloat16
F32 = jnp.float32


def dot_nn(a, b):
    return lax.dot_general(a, b, (((1,), (0,)), ((), ())), preferred_element_type=F32)


def dot_nt(a, b):
    return lax.dot_general(a, b, (((1,), (1,)), ((), ())), preferred_element_type=F32)


def dot_tn(a, b):
    return lax.dot_general(a, b, (((0,), (0,)), ((), ())), preferred_element_type=F32)


def norm_forward(values, gain, bias):
    mean_row = jnp.mean(values, -1, keepdims=True)
    centred = values - mean_row
    spread = jnp.mean(centred * centred, -1, keepdims=True)
    scale_row = lax.rsqrt(spread + eps_norm)
    normal = centred * scale_row
    return (normal * gain + bias, normal, scale_row)


def norm_backward(grad_out, normal, scale_row, gain):
    grad_normal = grad_out * gain
    first_term = jnp.mean(grad_normal, -1, keepdims=True)
    second_term = jnp.mean(grad_normal * normal, -1, keepdims=True)
    grad_in = scale_row * (grad_normal - first_term - normal * second_term)
    return (grad_in, jnp.sum(grad_out * normal, 0), jnp.sum(grad_out, 0))


def gelu_exact(values):
    return jax.nn.gelu(values, approximate=False)


def adam_update(master, first, second, grad, rate, decay):
    moment = beta_one * first + (1.0 - beta_one) * grad
    square = beta_two * second + (1.0 - beta_two) * grad * grad
    step_size = (
        moment / (1.0 - beta_one**STEP) / (jnp.sqrt(square / (1.0 - beta_two**STEP)) + eps_adam)
    )
    updated = master - rate * (step_size + decay * master)
    return (updated, moment, square)


LOG2E = 1.4426950408889634


def _halves(ref_value):
    lane = lax.broadcasted_iota(jnp.int32, ref_value.shape, 1)
    zero = jnp.zeros_like(ref_value)
    return (jnp.where(lane < HEAD_DIM, ref_value, zero), jnp.where(lane >= HEAD_DIM, ref_value, zero))


def _scores(k_chunk, q_half, base, starts, places):
    s = dot_nt(k_chunk, q_half) * (LOG2E * HEAD_DIM ** (-0.5))
    key = base + lax.broadcasted_iota(jnp.int32, s.shape, 0)
    return jnp.where((key >= starts) & (key <= places), s, blocked)


def attend_forward_kernel(rows, halo, lows, q_ref, k_ref, v_ref, starts_ref, out_ref, lse_ref, vt_ref):
    window = rows + halo
    block = min(256, rows)
    vt_ref[...] = v_ref[...].T
    for b in range(rows // block):
        q = q_ref[pl.ds(b * block, block), :]
        halves = _halves(q)
        starts = starts_ref[:, pl.ds(b * block, block)]
        places = halo + b * block + lax.broadcasted_iota(jnp.int32, (1, block), 1)

        def step(c, carry):
            base = pl.multiple_of(c * KEYS, KEYS)
            k_chunk = k_ref[pl.ds(base, KEYS), :]
            new = []
            for h in range(2):
                peak, total, acc = carry[3 * h : 3 * h + 3]
                s = _scores(k_chunk, halves[h], base, starts, places)
                peak_new = jnp.maximum(peak, jnp.max(s, 0, keepdims=True))
                fade = jnp.exp2(peak - peak_new)
                raised = jnp.exp2(s - peak_new)
                total = total * fade + jnp.sum(raised, 0, keepdims=True)
                vt = vt_ref[h * HEAD_DIM : (h + 1) * HEAD_DIM, pl.ds(base, KEYS)]
                acc = acc * fade + dot_nn(vt, raised.astype(BF))
                new += [peak_new, total, acc]
            return tuple(new)

        zero = (
            jnp.full((1, block), blocked, F32),
            jnp.zeros((1, block), F32),
            jnp.zeros((HEAD_DIM, block), F32),
        )
        last = -(-(halo + (b + 1) * block) // KEYS)
        got = lax.fori_loop(lows[b], last, step, zero + zero)
        for h in range(2):
            peak, total, acc = got[3 * h : 3 * h + 3]
            out_ref[h * HEAD_DIM : (h + 1) * HEAD_DIM, pl.ds(b * block, block)] = acc / total
            lse_ref[0, h : h + 1, pl.ds(b * block, block)] = peak + jnp.log2(total)


def attend_forward(q, kv, starts, lows):
    rows, window = q.shape[0], kv.shape[0]
    halo = window - rows
    pairs = q.shape[1] // 128

    def kernel(lows_ref, *refs):
        attend_forward_kernel(rows, halo, lows_ref, *refs)

    return pl.pallas_call(
        kernel,
        grid_spec=pltpu.PrefetchScalarGridSpec(
            num_scalar_prefetch=1,
            grid=(pairs,),
            in_specs=[
                pl.BlockSpec((rows, 128), lambda p, lows: (0, p)),
                pl.BlockSpec((window, 128), lambda p, lows: (0, p)),
                pl.BlockSpec((window, 128), lambda p, lows: (0, pairs + p)),
                pl.BlockSpec((1, rows), lambda p, lows: (0, 0)),
            ],
            out_specs=[
                pl.BlockSpec((128, rows), lambda p, lows: (p, 0)),
                pl.BlockSpec((1, 2, rows), lambda p, lows: (p, 0, 0)),
            ],
            scratch_shapes=[pltpu.VMEM((128, window), BF)],
        ),
        out_shape=[
            jax.ShapeDtypeStruct((q.shape[1], rows), F32),
            jax.ShapeDtypeStruct((pairs, 2, rows), F32),
        ],
        cost_estimate=pl.CostEstimate(
            flops=4 * rows * window * q.shape[1], bytes_accessed=16 << 20, transcendentals=0
        ),
        compiler_params=pltpu.CompilerParams(vmem_limit_bytes=40 << 20),
    )(lows, q, kv, kv, starts)


def attend_backward_kernel(
    rows, halo, lows, q_ref, k_ref, v_ref, g_ref, out_ref, lse_ref, starts_ref,
    gq_ref, gkv_ref, kt_ref, gk_acc, gv_acc,
):
    block = min(256, rows)
    kt_ref[...] = k_ref[...].T
    gk_acc[...] = jnp.zeros_like(gk_acc)
    gv_acc[...] = jnp.zeros_like(gv_acc)
    scale = HEAD_DIM ** (-0.5)
    for b in range(rows // block):
        span = pl.ds(b * block, block)
        q = q_ref[span, :]
        g = g_ref[span, :]
        q_halves, g_halves = _halves(q), _halves(g)
        q_stack = jnp.concatenate(q_halves, 0)
        g_stack = jnp.concatenate(g_halves, 0)
        starts = starts_ref[:, span]
        places = halo + b * block + lax.broadcasted_iota(jnp.int32, (1, block), 1)
        product = g.astype(F32).T * out_ref[:, span]
        deltas = [
            jnp.sum(product[h * HEAD_DIM : (h + 1) * HEAD_DIM], 0, keepdims=True) for h in range(2)
        ]
        lses = [lse_ref[0, h : h + 1, span] for h in range(2)]

        def step(c, carry):
            base = pl.multiple_of(c * KEYS, KEYS)
            here = pl.ds(base, KEYS)
            k_chunk = k_ref[here, :]
            v_chunk = v_ref[here, :]
            shares, scores, new = [], [], []
            for h in range(2):
                s = _scores(k_chunk, q_halves[h], base, starts, places)
                share = jnp.exp2(s - lses[h])
                grad_share = dot_nt(v_chunk, g_halves[h])
                grad_score = (share * (grad_share - deltas[h])).astype(BF)
                shares.append(share.astype(BF))
                scores.append(grad_score)
                kt = kt_ref[h * HEAD_DIM : (h + 1) * HEAD_DIM, here]
                new.append(carry[h] + dot_nn(kt, grad_score))
            gk_acc[here, :] += dot_nn(jnp.concatenate(scores, 1), q_stack)
            gv_acc[here, :] += dot_nn(jnp.concatenate(shares, 1), g_stack)
            return tuple(new)

        zero = jnp.zeros((HEAD_DIM, block), F32)
        last = -(-(halo + (b + 1) * block) // KEYS)
        got = lax.fori_loop(lows[b], last, step, (zero, zero))
        gq_ref[span, :] = (jnp.concatenate(got, 0).T * scale).astype(BF)
    gkv_ref[0] = (gk_acc[...] * scale).astype(BF)
    gkv_ref[1] = gv_acc[...].astype(BF)


def attend_backward(q, kv, grad_attended, out_t, lse, starts, lows):
    rows, window = q.shape[0], kv.shape[0]
    halo = window - rows
    pairs = q.shape[1] // 128

    def kernel(lows_ref, *refs):
        attend_backward_kernel(rows, halo, lows_ref, *refs)

    return pl.pallas_call(
        kernel,
        grid_spec=pltpu.PrefetchScalarGridSpec(
            num_scalar_prefetch=1,
            grid=(pairs,),
            in_specs=[
                pl.BlockSpec((rows, 128), lambda p, lows: (0, p)),
                pl.BlockSpec((window, 128), lambda p, lows: (0, p)),
                pl.BlockSpec((window, 128), lambda p, lows: (0, pairs + p)),
                pl.BlockSpec((rows, 128), lambda p, lows: (0, p)),
                pl.BlockSpec((128, rows), lambda p, lows: (p, 0)),
                pl.BlockSpec((1, 2, rows), lambda p, lows: (p, 0, 0)),
                pl.BlockSpec((1, rows), lambda p, lows: (0, 0)),
            ],
            out_specs=[
                pl.BlockSpec((rows, 128), lambda p, lows: (0, p)),
                pl.BlockSpec((2, window, 128), lambda p, lows: (0, 0, p)),
            ],
            scratch_shapes=[
                pltpu.VMEM((128, window), BF),
                pltpu.VMEM((window, 128), F32),
                pltpu.VMEM((window, 128), F32),
            ],
        ),
        out_shape=[
            jax.ShapeDtypeStruct(q.shape, BF),
            jax.ShapeDtypeStruct((2, window, q.shape[1]), BF),
        ],
        cost_estimate=pl.CostEstimate(
            flops=10 * rows * window * q.shape[1], bytes_accessed=24 << 20, transcendentals=0
        ),
        compiler_params=pltpu.CompilerParams(vmem_limit_bytes=40 << 20),
    )(lows, q, kv, kv, grad_attended, out_t, lse, starts)


def gather_matrix(shard):
    whole = lax.all_gather(shard.astype(BF), "tensor", axis=shard.ndim - 1, tiled=True)
    return lax.all_gather(whole, "dp", axis=0, tiled=True)


def scatter_matrix(grad):
    part = lax.psum_scatter(grad, "dp", scatter_dimension=0, tiled=True)
    return lax.psum_scatter(part, "tensor", scatter_dimension=grad.ndim - 1, tiled=True).astype(F32)


def from_before(value):
    n = lax.axis_size("tensor")
    return lax.ppermute(value, "tensor", [(i, i + 1) for i in range(n - 1)])


def to_before(value):
    n = lax.axis_size("tensor")
    return lax.ppermute(value, "tensor", [(i + 1, i) for i in range(n - 1)])


def body(
    tokens,
    out_grad,
    seq_lengths,
    master_qkv,
    first_qkv,
    second_qkv,
    master_mix,
    first_mix,
    second_mix,
    master_up,
    first_up,
    second_up,
    master_down,
    first_down,
    second_down,
    master_norms,
    first_norms,
    second_norms,
    master_midnorm,
    first_midnorm,
    second_midnorm,
    master_heads,
    first_heads,
    second_heads,
):
    parts = lax.axis_size("tensor")
    place = lax.axis_index("tensor")
    rows, model = tokens.shape
    hops = min(-(-(LONGEST - 1) // rows), parts - 1)
    halo = hops * rows
    block = min(256, rows)

    ends = jnp.cumsum(seq_lengths[0])
    places = place * rows + jnp.arange(rows, dtype=jnp.int32)
    begun = jnp.where(places[:, None] >= ends[None, :], ends[None, :], 0)
    starts = jnp.max(begun, 1).astype(jnp.int32) - place * rows + halo
    lows = starts[::block] // KEYS
    starts = starts[None, :]

    w_qkv = gather_matrix(master_qkv).reshape(model, 3 * model)
    w_mix = gather_matrix(master_mix)
    w_up = gather_matrix(master_up)
    w_down = gather_matrix(master_down)
    w_q, w_kv = w_qkv[:, :model], w_qkv[:, model:]

    inputs = tokens.astype(F32)
    normed_one, normal_one, scale_one = norm_forward(inputs, master_norms[0], master_norms[1])
    normed_one = normed_one.astype(BF)
    window = [normed_one]
    for _ in range(hops):
        window.insert(0, from_before(window[0]))
    window = jnp.concatenate(window, 0)
    queries = dot_nn(normed_one, w_q).astype(BF)
    keys_values = dot_nn(window, w_kv).astype(BF)
    out_t, lse = attend_forward(queries, keys_values, starts, lows)
    attended = out_t.T
    gains = jnp.repeat(master_heads, HEAD_DIM)
    scaled = (attended * gains[None, :]).astype(BF)
    mixed = dot_nt(scaled, w_mix)
    post, normal_two, scale_two = norm_forward(mixed, master_norms[2], master_norms[3])
    hidden = inputs + post
    normed_three, normal_three, scale_three = norm_forward(hidden, master_norms[4], master_norms[5])
    normed_three = normed_three.astype(BF)
    upper = dot_nn(normed_three, w_up)
    activated, gelu_back = jax.vjp(gelu_exact, upper)
    mean_row = jnp.sum(activated, 1, keepdims=True) / FF
    spread = jnp.sum(activated * activated, 1, keepdims=True) / FF - mean_row * mean_row
    scale_mid = lax.rsqrt(spread + eps_norm)
    normal_mid = (activated - mean_row) * scale_mid
    reshaped = (normal_mid * master_midnorm[0] + master_midnorm[1]).astype(BF)
    layer_out = (hidden + dot_nt(reshaped, w_down)).astype(BF)

    grad_down = dot_tn(out_grad, reshaped).astype(BF)
    shard_down = scatter_matrix(grad_down)
    grad_reshaped = dot_nn(out_grad, w_down)
    grad_normal_mid = grad_reshaped * master_midnorm[0]
    sum_one = jnp.sum(grad_normal_mid, 1, keepdims=True) / FF
    sum_two = jnp.sum(grad_normal_mid * normal_mid, 1, keepdims=True) / FF
    grad_activated = scale_mid * (grad_normal_mid - sum_one - normal_mid * sum_two)
    grad_upper = gelu_back(grad_activated)[0].astype(BF)
    grad_midnorm = jnp.stack([jnp.sum(grad_reshaped * normal_mid, 0), jnp.sum(grad_reshaped, 0)])
    grad_up = dot_tn(normed_three, grad_upper).astype(BF)
    shard_up = scatter_matrix(grad_up)
    grad_normed_three = dot_nt(grad_upper, w_up)
    grad_hidden_ffn, grad_gain_three, grad_bias_three = norm_backward(
        grad_normed_three, normal_three, scale_three, master_norms[4]
    )
    grad_hidden = out_grad.astype(F32) + grad_hidden_ffn
    grad_mixed, grad_gain_two, grad_bias_two = norm_backward(
        grad_hidden, normal_two, scale_two, master_norms[2]
    )
    grad_mixed = grad_mixed.astype(BF)
    grad_scaled = dot_nn(grad_mixed, w_mix)
    grad_mix = dot_tn(grad_mixed, scaled).astype(BF)
    shard_mix = scatter_matrix(grad_mix)
    grad_heads = jnp.sum((grad_scaled * attended).reshape(rows, HEADS, HEAD_DIM), (0, 2))
    grad_attended = (grad_scaled * gains[None, :]).astype(BF)
    grad_q, grad_kv = attend_backward(queries, keys_values, grad_attended, out_t, lse, starts, lows)
    grad_k, grad_v = grad_kv[0], grad_kv[1]
    grad_window = dot_nt(grad_k, w_kv[:, :model]) + dot_nt(grad_v, w_kv[:, model:])
    back = None
    for hop in range(hops):
        part = grad_window[hop * rows : (hop + 1) * rows]
        back = to_before((part if back is None else part + back).astype(BF)).astype(F32)
    grad_normed_one = grad_window[halo:] + dot_nt(grad_q, w_q)
    if back is not None:
        grad_normed_one = grad_normed_one + back
    grad_qkv = jnp.stack(
        [
            dot_tn(normed_one, grad_q).astype(BF),
            dot_tn(window, grad_k).astype(BF),
            dot_tn(window, grad_v).astype(BF),
        ],
        1,
    )
    shard_qkv = scatter_matrix(grad_qkv)
    grad_in, grad_gain_one, grad_bias_one = norm_backward(
        grad_normed_one, normal_one, scale_one, master_norms[0]
    )
    input_grad = grad_hidden + grad_in

    grad_norms = jnp.stack(
        [
            grad_gain_one,
            grad_bias_one,
            grad_gain_two,
            grad_bias_two,
            grad_gain_three,
            grad_bias_three,
        ]
    )
    grad_norms, grad_midnorm, grad_heads = lax.psum(
        (grad_norms, grad_midnorm, grad_heads), ("dp", "tensor")
    )
    new_qkv = adam_update(master_qkv, first_qkv, second_qkv, shard_qkv, rate_matrix, decay_matrix)
    new_mix = adam_update(master_mix, first_mix, second_mix, shard_mix, rate_matrix, decay_matrix)
    new_up = adam_update(master_up, first_up, second_up, shard_up, rate_matrix, decay_matrix)
    new_down = adam_update(
        master_down, first_down, second_down, shard_down, rate_matrix, decay_matrix
    )
    new_norms = adam_update(master_norms, first_norms, second_norms, grad_norms, rate_vector, 0.0)
    new_midnorm = adam_update(
        master_midnorm, first_midnorm, second_midnorm, grad_midnorm, rate_vector, 0.0
    )
    new_heads = adam_update(master_heads, first_heads, second_heads, grad_heads, rate_vector, 0.0)
    return (
        (layer_out, input_grad)
        + new_qkv
        + new_mix
        + new_up
        + new_down
        + new_norms
        + new_midnorm
        + new_heads
    )


def solution(mesh):
    token, matrix, cube = P(("dp", "tensor"), None), P("dp", "tensor"), P("dp", None, "tensor")
    in_specs = (token, token, P("dp", None)) + (cube,) * 3 + (matrix,) * 9 + (P(),) * 9
    out_specs = (token, token) + (cube,) * 3 + (matrix,) * 9 + (P(),) * 9
    return jax.shard_map(body, mesh=mesh, in_specs=in_specs, out_specs=out_specs, check_vma=False)
```

time: 1590 us -> 763 us (0.48)
  waiting for transfers between devices: 963 us -> 394 us
  matrix products: 256 us -> 125 us
  local copies, waits for them, and re-layouts: 138 us -> 11.8 us
  other arithmetic: 113 us -> 46.4 us
  Pallas kernels: 0 us -> 49.3 us
    reduce_scatter x8, waiting for transfers between devices: 615 us -> 210 us  [the longest x4 116 us: scatter_matrix(): part = lax.psum_scatter(grad, 'dp', scatter_dimension=0, tiled=True)]
    all_gather x7 -> x6, waiting for transfers between devices: 347 us -> 140 us  [the longest x4 113 us: gather_matrix(): return lax.all_gather(whole, 'dp', axis=0, tiled=True)]
    dot_general x40 -> x17, matrix products: 256 us -> 125 us  [the longest x5 53.9 us: dot_nn(): lax.dot_general(a, b, (((1,), (0,)), ((), ())), preferred_element_type=F32)]
    dynamic_update_slice x17 -> x0, local copies, waits for them, and re-layouts: 67.7 us -> none  [the longest x16 66.5 us: attend_forward(): results, log_total = lax.map(one_block, jnp.arange(blocks, dtype=jnp.int32))]
    pallas_call x0 -> x2, Pallas kernels: none -> 49.3 us  [the longest x1 27.8 us: attend_backward(): pl.pallas_call(kernel, grid_spec=pltpu.PrefetchScalarGridSpec(num_scalar_...]
    ppermute x0 -> x4, waiting for transfers between devices: none -> 43.4 us  [the longest x2 26.3 us: to_before(): return lax.ppermute(value, 'tensor', [(i + 1, i) for i in range(n - 1)])]
    all_gather x1 -> x2, blocking collectives: 12.9 us -> 44.1 us  [gather_matrix(): lax.all_gather(shard.astype(BF), 'tensor', axis=shard.ndim - 1, tiled=True)]
    reduce_sum x7 -> x1, other arithmetic: 23.5 us -> 0.12 us  [body(): jnp.sum((grad_scaled * attended).reshape(rows, HEADS, HEAD_DIM), (0, 2))]
  transfers between devices with their start and end apart: 15 -> 18, of which waited for: 13 -> 13; matrix products, arithmetic and copies ran while one was open for 18% -> 12% of each run, Pallas kernels for 0% -> 7%
where the time goes in v1:
time: 763 us; the launch traced here: 755 us
  waiting for transfers between devices  394 us (52%)
  matrix products  125 us (16%)
  blocking collectives  99.7 us (13%)
  Pallas kernels  49.3 us (6%)
  other arithmetic  46.4 us (6%)
  between operations  15.1 us (2%)
  starting transfers between devices  13.7 us (2%)
  local copies, waits for them, and re-layouts  11.8 us (2%)
    reduce_scatter x4, waiting for transfers between devices, scatter_matrix(): part = lax.psum_scatter(grad, 'dp', scatter_dimension=0, tiled=True)  116 us
    all_gather x4, waiting for transfers between devices, gather_matrix(): return lax.all_gather(whole, 'dp', axis=0, tiled=True)  113 us
    reduce_scatter x4, waiting for transfers between devices, scatter_matrix(): lax.psum_scatter(part, 'tensor', scatter_dimension=grad.ndim - 1, tiled=T...  93.6 us
    psum x1, blocking collectives, body(): lax.psum((grad_norms, grad_midnorm, grad_heads), ('dp', 'tensor'))  55.6 us
    dot_general x5, matrix products, dot_nn(): lax.dot_general(a, b, (((1,), (0,)), ((), ())), preferred_element_type=F32)  53.9 us
    all_gather x2, blocking collectives, gather_matrix(): lax.all_gather(shard.astype(BF), 'tensor', axis=shard.ndim - 1, tiled=True)  44.1 us
    dot_general x6, matrix products, dot_nt(): lax.dot_general(a, b, (((1,), (1,)), ((), ())), preferred_element_type=F32)  39.5 us
    dot_general x6, matrix products, dot_tn(): lax.dot_general(a, b, (((0,), (0,)), ((), ())), preferred_element_type=F32)  31.5 us
  transfers between devices with their start and end apart: 18, of which 13 were waited for; matrix products, arithmetic and copies ran while one was open for 12% of the time, Pallas kernels for 7%

profile of v1, /device:TPU:0, one launch (start us, length us, event | category | flops | bytes accessed | tf_op | source)
XLA Modules:
  0.0 754.7 jit_solution(1554165864721436213)
XLA Ops:
  7.3 1.9 convert_element_type.99
  10.4 28.0 %all_gather.24 = bf16[128,3,1024]{0,2,1:T(8,128)(2,1)} all-gather(bf16[128,3,256]{0,2,1:T(8,128)(2,1)S(1)} %copy.52), channel_id=1, replica_groups=mesh['dp'=8,'tensor'=4] {'tensor'}, dimensions={2}, use_global_device_ids=true | all-gather | bytes 983040 | tf_op jit(solution)/shard_map/all_gather | solution.py:259
  39.4 16.1 %all_gather.26 = bf16[128,1024]{1,0:T(8,128)(2,1)} all-gather(bf16[128,256]{1,0:T(8,128)(2,1)S(1)} %convert_element_type.97), channel_id=1, replica_groups=mesh['dp'=8,'tensor'=4] {'tensor'}, dimensions={1}, use_global_device_ids=true | all-gather | bytes 327680 | tf_op jit(solution)/shard_map/all_gather | solution.py:259
  57.3 4.4 collective-permute-start
  62.3 17.1 %collective-permute-done = bf16[512,1024]{1,0:T(8,128)(2,1)} collective-permute-done((bf16[512,1024]{1,0:T(8,128)(2,1)S(1)}, bf16[512,1024]{1,0:T(8,128)(2,1)}, u32[]{:S(2)}, u32[]{:S(2)}) %collective-permute-start) | collective-permute-done | bytes 1048608 | tf_op jit(solution)/shard_map/ppermute | solution.py:270
  79.4 5.5 collective-permute-start.1
  84.9 13.3 %all-gather.7.cloned.1.call-done = bf16[1024,3,1024]{0,2,1:T(8,128)(2,1)} async-done(((bf16[128,3,1024]{0,2,1:T(8,128)(2,1)}), bf16[1024,3,1024]{0,2,1:T(8,128)(2,1)}) %all-gather.7.cloned.1.call-update) | async-done | bytes 6291472 | tf_op jit(solution)/shard_map/all_gather | solution.py:260
  98.2 3.0 fusion.46.refs_0_
  101.6 8.6 %convolution_convert_fusion.1.refs_1_.refs_2_ = bf16[1536,2048]{1,0:T(8,128)(2,1)S(1)} fusion(bf16[1024,3072]{0,1:T(8,128)(2,1)S(1)} %bitcast.104, bf16[512,1024]{1,0:T(8,128)(2,1)S(1)} %fusion.25, bf16[512,1024]{1,0:T(8,128)(2,1)} %collective-permute-done, bf16[512,1024]{1,0:T(8,128)(2,1)} %collective-permute-done.1), kind=kOutput, calls=%fused_computation.24 | convolution fusion | flops 6455033856 | bytes 13631488 | tf_op jit(solution)/shard_map/dot_general | solution.py:32
  110.2 21.4 %shard_map.407 = (f32[1024,512]{1,0:T(8,128)S(1)}, f32[8,2,512]{2,1,0:T(2,128)S(1)}) custom-call(s32[2]{0:T(128)S(1)} %and_select_fusion.lows_ref, bf16[512,1024]{1,0:T(8,128)(2,1)S(1)} %fusion.46.refs_0_, bf16[1536,2048]{1,0:T(8,128)(2,1)S(1)} %convolution_convert_fusion.1.refs_1_.refs_2_, bf16[1536,2048]{1,0:T(8,128)(2,1)S(1)} %convolution_convert_fusion.1.refs_1_.refs_2_, ...), custom_call_target="tpu_custom_call" | custom-call | flops 3221225472 | bytes 16777216 | tf_op jit(solution)/shard_map/pallas_call | solution.py:136
  131.6 1.8 copy.53
  133.4 3.7 fusion.81
  139.9 44.4 %all-gather.13.cloned.1.call-done = bf16[1024,4096]{1,0:T(8,128)(2,1)} async-done(((bf16[128,4096]{1,0:T(8,128)(2,1)}), bf16[1024,4096]{1,0:T(8,128)(2,1)}) %all-gather.13.cloned.1.call-update) | async-done | bytes 8388624 | tf_op jit(solution)/shard_map/all_gather | solution.py:260
  184.3 28.7 %fusion.64 = (f32[512]{0:T(512)S(1)}, f32[512]{0:T(512)S(1)}, f32[512,4096]{1,0:T(8,128)S(1)}, f32[512,4096]{1,0:T(8,128)}, f32[512,4096]{1,0:T(8,128)}) fusion(bf16[1024,4096]{1,0:T(8,128)(2,1)} %all-gather.13.cloned.1.call-done, f32[512,1024]{1,0:T(8,128)} %copy-done.9, f32[1024]{0:T(1024)S(1)} %bitcast.97, f32[1024]{0:T(1024)S(1)} %bitcast.85, ...), kind=kOutput, calls=%fused_computation.152 | convolution fusion | flops 4438096896 | bytes 35667968 | tf_op jit(solution)/shard_map/dot_general | solution.py:32
  213.0 3.2 copy-done.14
  216.2 7.1 convert_bitcast_fusion
  223.4 71.4 %reduce-scatter.21.cloned.1.call-done = bf16[128,4096]{1,0:T(8,128)(2,1)} async-done(((bf16[1024,4096]{1,0:T(8,128)(2,1)}), bf16[128,4096]{1,0:T(8,128)(2,1)}) %reduce-scatter.21.cloned.1.call-update) | async-done | bytes 1048592 | tf_op jit(solution)/shard_map/reduce_scatter | solution.py:264
  294.9 29.4 %reduce-scatter.23.cloned.1.call-done = bf16[128,1024]{1,0:T(8,128)(2,1)} async-done(((bf16[128,4096]{1,0:T(8,128)(2,1)}), bf16[128,1024]{1,0:T(8,128)(2,1)}) %reduce-scatter.23.cloned.1.call-update) | async-done | bytes 262160 | tf_op jit(solution)/shard_map/reduce_scatter | solution.py:265
  324.2 3.1 multiply_subtract_fusion
  327.4 26.7 %all-gather.15.cloned.1.call-done = bf16[128,4096]{1,0:T(8,128)(2,1)} async-done(((bf16[128,1024]{1,0:T(8,128)(2,1)}), bf16[128,4096]{1,0:T(8,128)(2,1)}) %all-gather.15.cloned.1.call-update) | async-done | bytes 1048592 | tf_op jit(solution)/shard_map/all_gather | solution.py:259
  354.1 55.7 %all-gather.17.cloned.1.call-done = bf16[1024,4096]{1,0:T(8,128)(2,1)} async-done(((bf16[128,4096]{1,0:T(8,128)(2,1)}), bf16[1024,4096]{1,0:T(8,128)(2,1)}) %all-gather.17.cloned.1.call-update) | async-done | bytes 8388624 | tf_op jit(solution)/shard_map/all_gather | solution.py:260
  409.9 9.9 %multiply_reduce_fusion = (f32[4096]{0:T(1024)S(1)}, f32[512]{0:T(512)S(1)}, f32[512]{0:T(512)S(1)}, f32[4096]{0:T(1024)S(1)}, f32[512,4096]{1,0:T(8,128)S(1)}) fusion(f32[512,4096]{1,0:T(8,128)} %copy-done.14, f32[512]{0:T(512)S(1)} %get-tuple-element.91, f32[512]{0:T(512)S(1)} %get-tuple-element.90, f32[4096]{0:T(1024)S(1)} %bitcast.75, ...), kind=kOutput, calls=%fused_computation.2 | convolution fusion | flops 4313832448 | bytes 26271744 | tf_op jit(solution)/shard_map/dot_general | solution.py:32
  419.8 12.8 %add_convert_fusion = bf16[512,4096]{1,0:T(8,128)(2,1)} fusion(f32[512,4096]{1,0:T(8,128)} %get-tuple-element.76, f32[512,4096]{1,0:T(8,128)} %get-tuple-element.94, f32[512,4096]{1,0:T(8,128)S(1)} %get-tuple-element.95, f32[512,4096]{1,0:T(8,128)} %copy-done.14, f32[512]{0:T(512)S(1)} %get-tuple-element.97, f32[512]{0:T(512)S(1)} %get-tuple-element.98, ...), kind=kLoop, calls=%fused_computation.4 | loop fusion | flops 44040192 | bytes 37773312 | tf_op jit(solution)/shard_map/convert_element_type | solution.py:358
  432.6 8.9 %multiply_reduce_fusion.4 = (f32[1024]{0:T(1024)S(1)}, f32[512]{0:T(512)S(1)}, f32[512]{0:T(512)S(1)}, f32[1024]{0:T(1024)S(1)}, f32[512,1024]{1,0:T(8,128)S(1)}) fusion(f32[512,1024]{1,0:T(8,128)S(1)} %copy-done.10, f32[512]{0:T(512)S(1)} %add_rsqrt_fusion.1, f32[512]{0:T(512)S(1)} %broadcast_multiply_fusion.9, f32[1024]{0:T(1024)S(1)} %bitcast.86, ...), kind=kOutput, calls=%fused_computation.69 | convolution fusion | flops 4299682816 | bytes 16797696 | tf_op jit(solution)/shard_map/dot_general | solution.py:36
  441.6 2.2 multiply_reduce_fusion.5
  446.3 2.6 convolution_convert_fusion.2
  449.2 3.8 fusion.37
  453.0 27.8 %shard_map.408 = (bf16[512,1024]{1,0:T(8,128)(2,1)S(1)}, bf16[2,1536,1024]{2,1,0:T(8,128)(2,1)S(1)}) custom-call(s32[2]{0:T(128)S(1)} %and_select_fusion.lows_ref, bf16[512,1024]{1,0:T(8,128)(2,1)S(1)} %fusion.46.refs_0_, bf16[1536,2048]{1,0:T(8,128)(2,1)} %copy-done, bf16[1536,2048]{1,0:T(8,128)(2,1)} %copy-done, ...), custom_call_target="tpu_custom_call" | custom-call | flops 8053063680 | bytes 25165824 | tf_op jit(solution)/shard_map/pallas_call | solution.py:223
  482.2 6.3 convert_bitcast_fusion.2
  488.5 5.1 convert_bitcast_fusion.1
  493.6 3.1 pad_maximum_fusion
  498.3 9.2 %convolution_convert_fusion = bf16[1024,4096]{1,0:T(8,128)(2,1)} fusion(bf16[512,4096]{1,0:T(8,128)(2,1)} %add_convert_fusion, f32[512,1024]{1,0:T(8,128)S(1)} %copy-done.11, f32[1024]{0:T(1024)S(1)} %bitcast.98, f32[1024]{0:T(1024)S(1)} %bitcast.88, f32[512]{0:T(512)S(1)} %add_rsqrt_fusion.1, f32[512]{0:T(512)S(1)} %broadcast_multiply_fusion.9), kind=kOutput, calls=%fused_computation.23 | convolution fusion | flops 4301783040 | bytes 14692352 | tf_op jit(solution)/shard_map/dot_general | solution.py:40
  507.5 6.1 fusion.12
  513.6 6.0 convolution_add_fusion
  521.1 26.3 %collective-permute-done.2 = bf16[512,1024]{1,0:T(8,128)(2,1)S(1)} collective-permute-done((bf16[512,1024]{1,0:T(8,128)(2,1)S(1)}, bf16[512,1024]{1,0:T(8,128)(2,1)S(1)}, u32[]{:S(2)}, u32[]{:S(2)}) %collective-permute-start.2) | collective-permute-done | bytes 1048608 | tf_op jit(solution)/shard_map/ppermute | solution.py:275
  550.4 11.9 %add_convert_fusion.2 = bf16[512,1024]{1,0:T(8,128)(2,1)} fusion(f32[512,1024]{1,0:T(8,128)} %copy-done.9, bf16[1024,4096]{1,0:T(8,128)(2,1)} %all-gather.17.cloned.1.call-done, f32[512,4096]{1,0:T(8,128)} %copy-done.14, f32[4096]{0:T(1024)S(1)} %bitcast.91, f32[4096]{0:T(1024)S(1)} %bitcast.77, f32[512]{0:T(512)S(1)} %get-tuple-element.91, ...), kind=kOutput, calls=%fused_computation.79 | convolution fusion | flops 4306501632 | bytes 19959808 | tf_op jit(solution)/shard_map/dot_general | solution.py:36
  562.5 32.9 %reduce-scatter.9.cloned.1.call-done = bf16[128,3,1024]{2,0,1:T(8,128)(2,1)} async-done(((bf16[1024,3,1024]{2,0,1:T(8,128)(2,1)}), bf16[128,3,1024]{2,0,1:T(8,128)(2,1)}) %reduce-scatter.9.cloned.1.call-update) | async-done | bytes 786448 | tf_op jit(solution)/shard_map/reduce_scatter | solution.py:264
  595.5 2.8 fusion.42
  598.5 4.2 fusion.30
  602.7 55.6 %all-reduce = (f32[6,1024]{1,0:T(8,128)S(1)}, f32[2,4096]{1,0:T(2,128)}, f32[16]{0:T(128)S(1)}) all-reduce(f32[6,1024]{1,0:T(8,128)S(1)} %stack.52, f32[2,4096]{1,0:T(2,128)S(1)} %pad_maximum_fusion.2, f32[16]{0:T(128)S(1)} %reduce_sum.258), channel_id=1, replica_groups=mesh['dp'=8,'tensor'=4] {'dp','tensor'}, use_global_device_ids=true, to_apply=%region_32.33 | all-reduce | flops 14352 | bytes 114816 | tf_op jit(solution)/shard_map/psum | solution.py:410
  658.9 11.7 %reduce-scatter.17.cloned.1.call-done = bf16[128,4096]{1,0:T(8,128)(2,1)} async-done(((bf16[1024,4096]{1,0:T(8,128)(2,1)}), bf16[128,4096]{1,0:T(8,128)(2,1)}) %reduce-scatter.17.cloned.1.call-update) | async-done | bytes 1048592 | tf_op jit(solution)/shard_map/reduce_scatter | solution.py:264
  671.9 3.7 fusion.29
  676.4 16.1 %reduce-scatter.15.cloned.1.call-done = bf16[128,256]{1,0:T(8,128)(2,1)} async-done(((bf16[128,1024]{1,0:T(8,128)(2,1)}), bf16[128,256]{1,0:T(8,128)(2,1)}) %reduce-scatter.15.cloned.1.call-update) | async-done | bytes 65552 | tf_op jit(solution)/shard_map/reduce_scatter | solution.py:265
  692.4 1.9 multiply_subtract_fusion.3
  694.3 22.1 %reduce-scatter.11.cloned.1.call-done = bf16[128,3,256]{2,0,1:T(8,128)(2,1)} async-done(((bf16[128,3,1024]{2,0,1:T(8,128)(2,1)}), bf16[128,3,256]{2,0,1:T(8,128)(2,1)}) %reduce-scatter.11.cloned.1.call-update) | async-done | bytes 196624 | tf_op jit(solution)/shard_map/reduce_scatter | solution.py:265
  716.3 2.4 multiply_subtract_fusion.2
  718.7 26.2 %reduce-scatter.19.cloned.1.call-done = bf16[128,1024]{1,0:T(8,128)(2,1)} async-done(((bf16[128,4096]{1,0:T(8,128)(2,1)}), bf16[128,1024]{1,0:T(8,128)(2,1)}) %reduce-scatter.19.cloned.1.call-update) | async-done | bytes 262160 | tf_op jit(solution)/shard_map/reduce_scatter | solution.py:265
  744.9 2.8 multiply_subtract_fusion.1
  (165 shorter events, 21.0 us)
Async XLA Ops:
  7.2 48.9 %copy-start.4 = (bf16[512,1024]{1,0:T(8,128)(2,1)S(1)}, bf16[512,1024]{1,0:T(8,128)(2,1)}, u32[]{:S(2)}) copy-start(bf16[512,1024]{1,0:T(8,128)(2,1)} %param.24) | copy-start | bytes 3145732
  7.2 49.6 %copy-start.25 = (f32[6,1024]{1,0:T(8,128)S(1)}, f32[6,1024]{1,0:T(8,128)}, u32[]{:S(2)}) copy-start(f32[6,1024]{1,0:T(8,128)} %param.39) | copy-start | bytes 73732
  7.2 48.4 %all-gather.11.cloned.1.call-start = ((), (), s32[]{:S(2)}) async-start(), calls=%async_computation.10 | async-start | bytes 1310720 | tf_op jit(solution)/shard_map/all_gather | solution.py:259
  9.1 52.6 %copy-start.43 = (s32[1,8]{1,0:T(1,128)S(1)}, s32[1,8]{1,0:T(1,128)}, u32[]{:S(2)}) copy-start(s32[1,8]{1,0:T(1,128)} %param.26) | copy-start | bytes 100
  9.2 53.0 %copy-start.38 = (f32[16]{0:T(128)S(1)}, f32[16]{0:T(128)}, u32[]{:S(2)}) copy-start(f32[16]{0:T(128)} %param.45) | copy-start | bytes 196
  9.2 75.7 %copy-start.23 = (f32[2,4096]{1,0:T(2,128)S(1)}, f32[2,4096]{1,0:T(2,128)}, u32[]{:S(2)}) copy-start(f32[2,4096]{1,0:T(2,128)} %param.42) | copy-start | bytes 98308
  9.2 89.0 %all-gather.7.cloned.1.call-start = ((), (), s32[]{:S(2)}) async-start(), calls=%async_computation.8 | async-start | bytes 7077888 | tf_op jit(solution)/shard_map/all_gather | solution.py:260
  38.4 95.0 %all-gather.9.cloned.1.call-start = ((), (), s32[]{:S(2)}) async-start(), calls=%async_computation.9 | async-start | bytes 2359296 | tf_op jit(solution)/shard_map/all_gather | solution.py:260
  55.5 128.8 %all-gather.13.cloned.1.call-start = ((), (), s32[]{:S(2)}) async-start(), calls=%async_computation.11 | async-start | bytes 9437184 | tf_op jit(solution)/shard_map/all_gather | solution.py:260
  56.1 238.7 %reduce-scatter.21.cloned.1.call-start = ((), (), s32[]{:S(2)}) async-start(), calls=%async_computation.20 | async-start | bytes 9437184 | tf_op jit(solution)/shard_map/reduce_scatter | solution.py:264
  56.4 41.8 %copy-start.29 = (f32[512]{0:T(512)}, f32[512]{0:T(512)S(1)}, u32[]{:S(2)}) copy-start(f32[512]{0:T(512)S(1)} %broadcast_multiply_fusion.11) | copy-start | bytes 6148
  56.8 44.4 %copy-start.36 = (f32[512]{0:T(512)}, f32[512]{0:T(512)S(1)}, u32[]{:S(2)}) copy-start(f32[512]{0:T(512)S(1)} %add_rsqrt_fusion.3) | copy-start | bytes 6148
  56.8 41.3 %copy-start.27 = (f32[1,1024]{1,0:T(1,128)}, f32[1,1024]{1,0:T(1,128)S(1)}, u32[]{:S(2)}) copy-start(f32[1,1024]{1,0:T(1,128)S(1)} %get-tuple-element.88) | copy-start | bytes 12292
  57.3 43.9 %copy-start.20 = (bf16[512,1024]{1,0:T(8,128)(2,1)}, bf16[512,1024]{1,0:T(8,128)(2,1)S(1)}, u32[]{:S(2)}) copy-start(bf16[512,1024]{1,0:T(8,128)(2,1)S(1)} %fusion.25) | copy-start | bytes 3145732
  57.3 22.1 %collective-permute-start = (bf16[512,1024]{1,0:T(8,128)(2,1)S(1)}, bf16[512,1024]{1,0:T(8,128)(2,1)}, u32[]{:S(2)}, u32[]{:S(2)}) collective-permute-start(bf16[512,1024]{1,0:T(8,128)(2,1)S(1)} %fusion.25), channel_id=1, source_target_pairs={{0,1},{1,2},{2,3},{4,5},{5,6},{6,7},{8,9},{9,10},{10,11},{12,13},{... | collective-permute-start | bytes 3145736 | tf_op jit(solution)/shard_map/ppermute | solution.py:270
  79.4 21.8 %collective-permute-start.1 = (bf16[512,1024]{1,0:T(8,128)(2,1)}, bf16[512,1024]{1,0:T(8,128)(2,1)}, u32[]{:S(2)}, u32[]{:S(2)}) collective-permute-start(bf16[512,1024]{1,0:T(8,128)(2,1)} %collective-permute-done), channel_id=1, source_target_pairs={{0,1},{1,2},{2,3},{4,5},{5,6},{6,7},{8,9},{9,10},{10,11},{12,13},{... | collective-permute-start | bytes 3145736 | tf_op jit(solution)/shard_map/ppermute | solution.py:270
  110.1 21.4 %copy-start = (bf16[1536,2048]{1,0:T(8,128)(2,1)}, bf16[1536,2048]{1,0:T(8,128)(2,1)S(1)}, u32[]{:S(2)}) copy-start(bf16[1536,2048]{1,0:T(8,128)(2,1)S(1)} %convolution_convert_fusion.1.refs_1_.refs_2_) | copy-start | bytes 18874372
  184.3 31.9 %copy-start.18 = (bf16[512,1024]{1,0:T(8,128)(2,1)S(1)}, bf16[512,1024]{1,0:T(8,128)(2,1)}, u32[]{:S(2)}) copy-start(bf16[512,1024]{1,0:T(8,128)(2,1)} %param.25) | copy-start | bytes 3145732
  223.3 100.9 %reduce-scatter.23.cloned.1.call-start = ((), (), s32[]{:S(2)}) async-start(), calls=%async_computation.21 | async-start | bytes 1310720 | tf_op jit(solution)/shard_map/reduce_scatter | solution.py:265
  294.8 59.2 %all-gather.15.cloned.1.call-start = ((), (), s32[]{:S(2)}) async-start(), calls=%async_computation.12 | async-start | bytes 1310720 | tf_op jit(solution)/shard_map/all_gather | solution.py:259
  327.3 82.5 %all-gather.17.cloned.1.call-start = ((), (), s32[]{:S(2)}) async-start(), calls=%async_computation.13 | async-start | bytes 9437184 | tf_op jit(solution)/shard_map/all_gather | solution.py:260
  354.1 196.0 %reduce-scatter.13.cloned.1.call-start = ((), (), s32[]{:S(2)}) async-start(), calls=%async_computation.16 | async-start | bytes 2359296 | tf_op jit(solution)/shard_map/reduce_scatter | solution.py:264
  419.8 12.8 %copy-start.10 = (f32[512,1024]{1,0:T(8,128)S(1)}, f32[512,1024]{1,0:T(8,128)}, u32[]{:S(2)}) copy-start(f32[512,1024]{1,0:T(8,128)} %copy-done.9) | copy-start | bytes 6291460
  432.6 9.0 %copy-start.8 = (f32[512,1024]{1,0:T(8,128)S(1)}, f32[512,1024]{1,0:T(8,128)}, u32[]{:S(2)}) copy-start(f32[512,1024]{1,0:T(8,128)} %copy-done.7) | copy-start | bytes 6291460
  432.6 9.0 %copy-start.19 = (bf16[512,1024]{1,0:T(8,128)(2,1)S(1)}, bf16[512,1024]{1,0:T(8,128)(2,1)}, u32[]{:S(2)}) copy-start(bf16[512,1024]{1,0:T(8,128)(2,1)} %param.25) | copy-start | bytes 3145732
  449.0 146.4 %reduce-scatter.9.cloned.1.call-start = ((), (), s32[]{:S(2)}) async-start(), calls=%async_computation.14 | async-start | bytes 7077888 | tf_op jit(solution)/shard_map/reduce_scatter | solution.py:264
  453.0 27.9 %copy-start.21 = (bf16[512,1024]{1,0:T(8,128)(2,1)S(1)}, bf16[512,1024]{1,0:T(8,128)(2,1)}, u32[]{:S(2)}) copy-start(bf16[512,1024]{1,0:T(8,128)(2,1)} %copy-done.20) | copy-start | bytes 3145732
  480.9 7.6 %copy-start.3 = (bf16[2,1536,1024]{2,1,0:T(8,128)(2,1)}, bf16[2,1536,1024]{2,1,0:T(8,128)(2,1)S(1)}, u32[]{:S(2)}) copy-start(bf16[2,1536,1024]{2,1,0:T(8,128)(2,1)S(1)} %get-tuple-element.29) | copy-start | bytes 18874372
  496.7 173.9 %reduce-scatter.17.cloned.1.call-start = ((), (), s32[]{:S(2)}) async-start(), calls=%async_computation.18 | async-start | bytes 9437184 | tf_op jit(solution)/shard_map/reduce_scatter | solution.py:264
  507.4 185.0 %reduce-scatter.15.cloned.1.call-start = ((), (), s32[]{:S(2)}) async-start(), calls=%async_computation.17 | async-start | bytes 327680 | tf_op jit(solution)/shard_map/reduce_scatter | solution.py:265
  519.6 27.8 %copy-start.15 = (f32[1536,1024]{1,0:T(8,128)}, f32[1536,1024]{1,0:T(8,128)S(1)}, u32[]{:S(2)}) copy-start(f32[1536,1024]{1,0:T(8,128)S(1)} %convolution_add_fusion) | copy-start | bytes 18874372
  519.8 27.6 %collective-permute-start.2 = (bf16[512,1024]{1,0:T(8,128)(2,1)S(1)}, bf16[512,1024]{1,0:T(8,128)(2,1)S(1)}, u32[]{:S(2)}, u32[]{:S(2)}) collective-permute-start(bf16[512,1024]{1,0:T(8,128)(2,1)S(1)} %slice.125), channel_id=1, source_target_pairs={{1,0},{2,1},{3,2},{5,4},{6,5},{7,6},{9,8},{10,9},{11,10},{13,12},{... | collective-permute-start | bytes 3145736 | tf_op jit(solution)/shard_map/ppermute | solution.py:275
  548.7 49.7 %collective-permute-start.3 = (bf16[512,1024]{1,0:T(8,128)(2,1)}, bf16[512,1024]{1,0:T(8,128)(2,1)}, u32[]{:S(2)}, u32[]{:S(2)}) collective-permute-start(bf16[512,1024]{1,0:T(8,128)(2,1)} %fusion.32), channel_id=1, source_target_pairs={{1,0},{2,1},{3,2},{5,4},{6,5},{7,6},{9,8},{10,9},{11,10},{13,12},{... | collective-permute-start | bytes 3145736 | tf_op jit(solution)/shard_map/ppermute | solution.py:275
  550.1 45.4 %copy-start.2 = (bf16[512,1024]{1,0:T(8,128)(2,1)S(1)}, bf16[512,1024]{1,0:T(8,128)(2,1)}, u32[]{:S(2)}) copy-start(bf16[512,1024]{1,0:T(8,128)(2,1)} %copy-done.1) | copy-start | bytes 3145732
  550.1 166.3 %reduce-scatter.11.cloned.1.call-start = ((), (), s32[]{:S(2)}) async-start(), calls=%async_computation.15 | async-start | bytes 983040 | tf_op jit(solution)/shard_map/reduce_scatter | solution.py:265
  562.3 36.2 %copy-start.6 = (bf16[512,1024]{1,0:T(8,128)(2,1)S(1)}, bf16[512,1024]{1,0:T(8,128)(2,1)}, u32[]{:S(2)}) copy-start(bf16[512,1024]{1,0:T(8,128)(2,1)} %param.24) | copy-start | bytes 3145732
  562.3 36.2 %copy-start.28 = (f32[1,1024]{1,0:T(1,128)S(1)}, f32[1,1024]{1,0:T(1,128)}, u32[]{:S(2)}) copy-start(f32[1,1024]{1,0:T(1,128)} %copy-done.27) | copy-start | bytes 12292
  562.3 36.2 %copy-start.30 = (f32[512]{0:T(512)S(1)}, f32[512]{0:T(512)}, u32[]{:S(2)}) copy-start(f32[512]{0:T(512)} %copy-done.29) | copy-start | bytes 6148
  562.3 36.2 %copy-start.37 = (f32[512]{0:T(512)S(1)}, f32[512]{0:T(512)}, u32[]{:S(2)}) copy-start(f32[512]{0:T(512)} %copy-done.36) | copy-start | bytes 6148
  595.4 149.5 %reduce-scatter.19.cloned.1.call-start = ((), (), s32[]{:S(2)}) async-start(), calls=%async_computation.19 | async-start | bytes 1310720 | tf_op jit(solution)/shard_map/reduce_scatter | solution.py:265
  598.4 72.3 %copy-start.39 = (f32[16]{0:T(128)S(1)}, f32[16]{0:T(128)}, u32[]{:S(2)}) copy-start(f32[16]{0:T(128)} %param.45) | copy-start | bytes 196
  598.4 72.3 %copy-start.40 = (f32[16]{0:T(128)S(1)}, f32[16]{0:T(128)}, u32[]{:S(2)}) copy-start(f32[16]{0:T(128)} %param.46) | copy-start | bytes 196
  598.4 72.3 %copy-start.41 = (f32[16]{0:T(128)S(1)}, f32[16]{0:T(128)}, u32[]{:S(2)}) copy-start(f32[16]{0:T(128)} %param.47) | copy-start | bytes 196
  598.4 72.9 %copy-start.26 = (f32[6,1024]{1,0:T(8,128)S(1)}, f32[6,1024]{1,0:T(8,128)}, u32[]{:S(2)}) copy-start(f32[6,1024]{1,0:T(8,128)} %param.39) | copy-start | bytes 73732
  598.4 72.9 %copy-start.31 = (f32[6,1024]{1,0:T(8,128)S(1)}, f32[6,1024]{1,0:T(8,128)}, u32[]{:S(2)}) copy-start(f32[6,1024]{1,0:T(8,128)} %param.40) | copy-start | bytes 73732
  598.4 72.9 %copy-start.32 = (f32[6,1024]{1,0:T(8,128)S(1)}, f32[6,1024]{1,0:T(8,128)}, u32[]{:S(2)}) copy-start(f32[6,1024]{1,0:T(8,128)} %param.41) | copy-start | bytes 73732
  598.4 73.5 %copy-start.13 = (f32[512,1024]{1,0:T(8,128)S(1)}, f32[512,1024]{1,0:T(8,128)}, u32[]{:S(2)}) copy-start(f32[512,1024]{1,0:T(8,128)} %copy-done.12) | copy-start | bytes 6291460
  671.9 44.4 %copy-start.17 = (f32[128,3,256]{2,0,1:T(8,128)S(1)}, f32[128,3,256]{2,0,1:T(8,128)}, u32[]{:S(2)}) copy-start(f32[128,3,256]{2,0,1:T(8,128)} %param.27) | copy-start | bytes 1179652
  (14 other events, 42.3 us)
Sparse Core Ops, SparseCore 0:
  10.2 39.2 all-gather.10
  51.3 46.7 all-gather.6
  100.1 27.9 all-gather.8
  129.8 54.4 all-gather.12
  223.5 71.2 reduce-scatter.20
  297.0 27.1 reduce-scatter.22
  327.4 26.5 all-gather.14
  355.9 53.8 all-gather.16
  449.1 41.2 reduce-scatter.12
  496.8 98.5 reduce-scatter.8
  598.9 71.7 reduce-scatter.16
  672.8 19.5 reduce-scatter.14
  694.7 21.5 reduce-scatter.10
  718.5 26.3 reduce-scatter.18
